TPU v7x, 256 devices: a whole 4x4x8 slice. The times are simulated.
256 devices in a mesh: wide: 16 (over x, z_lo), narrow: 16 (over z_hi, y, core).
Axes of the slice: x: 4, y: 4, z: 8 (z_hi: 2, z_lo: 4; z = z_hi * 4 + z_lo), core: 2. Of those that a mesh axis runs over, the one named last changes fastest.
Arguments:
- image_rows: bfloat16 [131072, 1152], P(('wide', 'narrow'))
- text_rows: bfloat16 [131072, 1152], P(('wide', 'narrow'))
- labels: int32 [131072], P(('wide', 'narrow')), may hold values from 0 to 511, as said below
- scale: float32 [1], replicated, may hold values from 3 to 12
- bias: float32 [1], replicated, may hold values from -4 to -1
Outputs:
- image_grad: float32 [131072, 1152], P(('wide', 'narrow'))
- text_grad: float32 [131072, 1152], P(('wide', 'narrow'))
- totals: float32 [3], replicated
Inputs may be any that keep to these rules, and one draw needn't show every extreme that they name: Within each group of 512 rows the labels are a permutation of the positions 0 to 511.
All inputs are finite; a program needn't handle non-finite values.
Results may differ from a plain program's by a relative error of at most 0.0006.
Values may be sent and summed in bfloat16 or wider, within the bound.
A program may use at most 128 MiB of HBM per device.

v0:
```python
import jax
import jax.numpy as jnp
from jax import lax
from jax.sharding import PartitionSpec as P

ROUNDS = 4


EPS = 1e-06


def from_partner(block, axis, distance):
    count = lax.axis_size(axis)
    route = []
    for low in range(count):
        high = low | 1 << distance
        if high != low and high < count:
            route += [(low, high), (high, low)]
    return lax.ppermute(block, axis, route)


def normalize(rows):
    values = rows.astype(jnp.float32)
    inverse = lax.rsqrt(jnp.sum(values * values, axis=-1, keepdims=True) + EPS)
    return (values * inverse, inverse)


def pair_block(image_part, text_part, target, scale_value, bias_value):
    cosine = lax.dot_general(
        image_part, text_part, (((1,), (1,)), ((), ())), preferred_element_type=jnp.float32
    )
    logit = scale_value * cosine + bias_value
    loss_part = jnp.sum(jax.nn.softplus(-target * logit))
    slope = -target * jax.nn.sigmoid(-target * logit)
    return (slope.astype(jnp.bfloat16), loss_part, jnp.sum(slope * cosine), jnp.sum(slope))


def image_side(slope_cast, text_part, scale_value):
    return scale_value * jnp.dot(slope_cast, text_part, preferred_element_type=jnp.float32)


def text_side(slope_cast, image_part, scale_value):
    return scale_value * lax.dot_general(
        slope_cast, image_part, (((0,), (0,)), ((), ())), preferred_element_type=jnp.float32
    )


def per_device(image_rows, text_rows, labels, scale, bias):
    row_count = image_rows.shape[0]
    scale_value = scale[0]
    bias_value = bias[0]
    image_unit, inv_image = normalize(image_rows)
    text_unit, inv_text = normalize(text_rows)
    image_cast = image_unit.astype(jnp.bfloat16)
    text_cast = text_unit.astype(jnp.bfloat16)
    positive = labels[:, None] == lax.broadcasted_iota(jnp.int32, (row_count, row_count), 1)
    own_target = jnp.where(positive, 1.0, -1.0).astype(jnp.float32)
    slope_cast, loss_sum, scale_sum, bias_sum = pair_block(
        image_cast, text_cast, own_target, scale_value, bias_value
    )
    image_acc = image_side(slope_cast, text_cast, scale_value)
    text_acc = text_side(slope_cast, image_cast, scale_value)
    far_target = jnp.float32(-1.0)
    levels = list(range(ROUNDS))
    for level in levels:
        partner_text = from_partner(text_cast, ("wide", "narrow"), level)
        slope_cast, loss_part, scale_part, bias_part = pair_block(
            image_cast, partner_text, far_target, scale_value, bias_value
        )
        image_acc = image_acc + image_side(slope_cast, partner_text, scale_value)
        outgoing = text_side(slope_cast, image_cast, scale_value)
        text_acc = text_acc + from_partner(outgoing, ("wide", "narrow"), level)
        loss_sum = loss_sum + loss_part
        scale_sum = scale_sum + scale_part
        bias_sum = bias_sum + bias_part
    image_grad = (
        image_acc - image_unit * jnp.sum(image_unit * image_acc, axis=-1, keepdims=True)
    ) * inv_image
    text_grad = (
        text_acc - text_unit * jnp.sum(text_unit * text_acc, axis=-1, keepdims=True)
    ) * inv_text
    loss_total, scale_total, bias_total = lax.psum(
        (loss_sum, scale_sum, bias_sum), ("wide", "narrow")
    )
    pair_count = row_count * lax.axis_size(("wide", "narrow"))
    totals = jnp.stack([loss_total, scale_total, bias_total]) / pair_count
    return (image_grad, text_grad, totals)


def solution(mesh):
    placed = (
        P(("wide", "narrow"), None),
        P(("wide", "narrow"), None),
        P(("wide", "narrow")),
        P(),
        P(),
    )
    return jax.shard_map(
        per_device,
        mesh=mesh,
        in_specs=placed,
        out_specs=(P(("wide", "narrow"), None), P(("wide", "narrow"), None), P()),
        check_vma=False,
    )
```

profile of v0, /device:TPU:2, one launch (start us, length us, event | category | flops | bytes accessed | tf_op | source)
XLA Modules:
  0.0 264.7 jit_solution(9762591036743902801)
XLA Ops:
  0.6 0.0 copy-start
  0.6 0.0 copy-start.9
  0.6 1.7 fusion.20
  2.3 1.5 fusion.9
  3.9 7.3 %collective-permute-start.3 = (bf16[512,1152]{1,0:T(8,128)(2,1)S(1)}, bf16[512,1152]{1,0:T(8,128)(2,1)S(1)}, u32[]{:S(2)}, u32[]{:S(2)}) collective-permute-start(bf16[512,1152]{1,0:T(8,128)(2,1)S(1)} %fusion.9), channel_id=1, source_target_pairs={{0,8},{8,0},{1,9},{9,1},{2,10},{10,2},{3,11},{11,3},{4,12},{12,4},... | collective-permute-start | bytes 3538952 | tf_op jit(solution)/shard_map/ppermute | solution.py:19
  11.1 3.2 %collective-permute-start.2 = (bf16[512,1152]{1,0:T(8,128)(2,1)S(1)}, bf16[512,1152]{1,0:T(8,128)(2,1)S(1)}, u32[]{:S(2)}, u32[]{:S(2)}) collective-permute-start(bf16[512,1152]{1,0:T(8,128)(2,1)S(1)} %fusion.9), channel_id=1, source_target_pairs={{0,4},{4,0},{1,5},{5,1},{2,6},{6,2},{3,7},{7,3},{8,12},{12,8},{9,1... | collective-permute-start | bytes 3538952 | tf_op jit(solution)/shard_map/ppermute | solution.py:19
  14.3 0.0 collective-permute-start
  14.3 0.7 collective-permute-start.1
  15.0 0.0 copy-done
  15.0 0.3 fusion.16
  16.6 0.0 copy-done.9
  16.7 2.6 fusion.21
  19.2 0.0 copy-start.5
  19.2 2.6 fusion.37
  21.9 0.0 copy-done.5
  21.9 39.3 %collective-permute-done.3 = bf16[512,1152]{1,0:T(8,128)(2,1)S(1)} collective-permute-done((bf16[512,1152]{1,0:T(8,128)(2,1)S(1)}, bf16[512,1152]{1,0:T(8,128)(2,1)S(1)}, u32[]{:S(2)}, u32[]{:S(2)}) %collective-permute-start.3) | collective-permute-done | bytes 1179680 | tf_op jit(solution)/shard_map/ppermute | solution.py:19
  61.2 2.4 fusion.25
  63.6 2.5 convolution_multiply_fusion
  66.1 6.6 %collective-permute-start.7 = (f32[512,1152]{1,0:T(8,128)}, f32[512,1152]{1,0:T(8,128)S(1)}, u32[]{:S(2)}, u32[]{:S(2)}) collective-permute-start(f32[512,1152]{1,0:T(8,128)} %convolution_multiply_fusion), channel_id=1, source_target_pairs={{0,8},{8,0},{1,9},{9,1},{2,10},{10,2},{3,11},{11,3},{4,12},{12,4},... | collective-permute-start | bytes 7077896 | tf_op jit(solution)/shard_map/ppermute | solution.py:19
  72.6 0.0 collective-permute-done.2
  72.6 0.0 copy-start.10
  72.6 2.4 fusion.24
  75.0 0.0 copy-done.10
  75.0 0.0 copy-start.16
  75.1 2.5 convolution_multiply_fusion.1
  77.5 0.0 copy-done.16
  77.5 3.2 %collective-permute-start.6 = (f32[512,1152]{1,0:T(8,128)}, f32[512,1152]{1,0:T(8,128)}, u32[]{:S(2)}, u32[]{:S(2)}) collective-permute-start(f32[512,1152]{1,0:T(8,128)} %convolution_multiply_fusion.1), channel_id=1, source_target_pairs={{0,4},{4,0},{1,5},{5,1},{2,6},{6,2},{3,7},{7,3},{8,12},{12,8},{9,1... | collective-permute-start | bytes 7077896 | tf_op jit(solution)/shard_map/ppermute | solution.py:19
  80.7 0.0 collective-permute-done.1
  80.7 0.0 copy-start.3
  80.7 2.4 fusion.23
  83.1 0.0 copy-done.3
  83.1 0.0 copy-start.7
  83.1 2.4 convolution_multiply_fusion.2
  85.6 0.0 copy-done.7
  85.6 0.7 collective-permute-start.5
  86.3 0.0 collective-permute-done
  86.3 0.0 copy-start.11
  86.3 2.4 fusion.22
  88.7 0.0 copy-done.11
  88.7 2.4 convolution_multiply_fusion.3
  91.1 0.0 copy-done.14
  91.1 0.0 collective-permute-start.4
  91.1 2.4 fusion.27
  103.0 143.9 %all-reduce = (f32[1]{0:T(128)}, f32[1]{0:T(128)}, f32[1]{0:T(128)}) all-reduce(f32[1]{0:T(128)} %bitcast.4, f32[1]{0:T(128)} %bitcast.3, f32[1]{0:T(128)} %bitcast.2), channel_id=1, replica_groups=mesh['wide'=16,'narrow'=16] {'wide','narrow'}, use_global_device_ids=true, to_apply=%region_21.22 | all-reduce | flops 3 | bytes 24 | tf_op jit(solution)/shard_map/psum | solution.py:82
  246.9 2.6 maximum_multiply_fusion
  249.5 2.7 %fusion.30 = f32[512,1152]{1,0:T(8,128)S(1)} fusion(bf16[512,1152]{1,0:T(8,128)(2,1)} %copy-done.10, f32[512,512]{1,0:T(8,128)} %copy-done.16, f32[]{:T(128)} %bitcast.37, f32[]{:T(128)} %bitcast.28), kind=kOutput, calls=%fused_computation.63 | convolution fusion | flops 605552640 | bytes 4587528 | tf_op jit(solution)/shard_map/dot_general | solution.py:39
  252.2 0.0 copy-done.12
  252.2 0.0 copy-done.13
  252.2 0.2 copy-done.15
  252.4 0.9 convolution_add_fusion.1
  253.3 0.8 copy-done.2
  254.1 0.3 copy-done.4
  254.4 0.3 copy-done.8
  254.7 1.1 fusion.13
  255.8 0.0 copy-start.6
  255.8 1.9 fusion.15
  257.7 0.0 collective-permute-done.7
  257.7 0.0 collective-permute-done.6
  257.7 0.0 collective-permute-done.5
  257.7 0.0 collective-permute-done.4
  257.7 0.0 copy-done.1
  257.7 0.1 copy-done.6
  257.9 5.0 %fusion.17 = (f32[512]{0:T(512)S(1)}, f32[512,1152]{1,0:T(8,128)S(1)}) fusion(bf16[512,1152]{1,0:T(8,128)(2,1)S(1)} %copy-done.1, f32[512]{0:T(512)S(1)} %add_rsqrt_fusion, f32[512,1152]{1,0:T(8,128)S(1)} %collective-permute-done.7, f32[512,1152]{1,0:T(8,128)} %collective-permute-done.6, f32[512,1152]{1,0:T(8,128)} %collective-permute-done.5, ...), kind=kOutput, calls=%fused_computation.33 | convolution fusion | flops 613940736 | bytes 15212552 | tf_op jit(solution)/shard_map/dot_general | solution.py:43
  262.8 1.9 fusion.19
  (10 shorter events, 0.0 us)
Async XLA Ops:
  0.6 14.4 %copy-start = (bf16[512,1152]{1,0:T(8,128)(2,1)S(1)}, bf16[512,1152]{1,0:T(8,128)(2,1)}, u32[]{:S(2)}) copy-start(bf16[512,1152]{1,0:T(8,128)(2,1)} %param.5) | copy-start | bytes 3538948
  0.6 16.0 %copy-start.9 = (s32[512]{0:T(512)S(1)}, s32[512]{0:T(512)}, u32[]{:S(2)}) copy-start(s32[512]{0:T(512)} %param.7) | copy-start | bytes 6148
  3.9 57.3 %collective-permute-start.3 = (bf16[512,1152]{1,0:T(8,128)(2,1)S(1)}, bf16[512,1152]{1,0:T(8,128)(2,1)S(1)}, u32[]{:S(2)}, u32[]{:S(2)}) collective-permute-start(bf16[512,1152]{1,0:T(8,128)(2,1)S(1)} %fusion.9), channel_id=1, source_target_pairs={{0,8},{8,0},{1,9},{9,1},{2,10},{10,2},{3,11},{11,3},{4,12},{12,4},... | collective-permute-start | bytes 3538952 | tf_op jit(solution)/shard_map/ppermute | solution.py:19
  11.1 61.5 %collective-permute-start.2 = (bf16[512,1152]{1,0:T(8,128)(2,1)S(1)}, bf16[512,1152]{1,0:T(8,128)(2,1)S(1)}, u32[]{:S(2)}, u32[]{:S(2)}) collective-permute-start(bf16[512,1152]{1,0:T(8,128)(2,1)S(1)} %fusion.9), channel_id=1, source_target_pairs={{0,4},{4,0},{1,5},{5,1},{2,6},{6,2},{3,7},{7,3},{8,12},{12,8},{9,1... | collective-permute-start | bytes 3538952 | tf_op jit(solution)/shard_map/ppermute | solution.py:19
  14.3 71.9 %collective-permute-start = (bf16[512,1152]{1,0:T(8,128)(2,1)S(1)}, bf16[512,1152]{1,0:T(8,128)(2,1)S(1)}, u32[]{:S(2)}, u32[]{:S(2)}) collective-permute-start(bf16[512,1152]{1,0:T(8,128)(2,1)S(1)} %fusion.9), channel_id=1, source_target_pairs={{0,1},{1,0},{2,3},{3,2},{4,5},{5,4},{6,7},{7,6},{8,9},{9,8},{10,11... | collective-permute-start | bytes 3538952 | tf_op jit(solution)/shard_map/ppermute | solution.py:19
  14.3 66.4 %collective-permute-start.1 = (bf16[512,1152]{1,0:T(8,128)(2,1)S(1)}, bf16[512,1152]{1,0:T(8,128)(2,1)S(1)}, u32[]{:S(2)}, u32[]{:S(2)}) collective-permute-start(bf16[512,1152]{1,0:T(8,128)(2,1)S(1)} %fusion.9), channel_id=1, source_target_pairs={{0,2},{2,0},{1,3},{3,1},{4,6},{6,4},{5,7},{7,5},{8,10},{10,8},{9,1... | collective-permute-start | bytes 3538952 | tf_op jit(solution)/shard_map/ppermute | solution.py:19
  19.2 2.6 copy-start.5
  66.1 191.7 %collective-permute-start.7 = (f32[512,1152]{1,0:T(8,128)}, f32[512,1152]{1,0:T(8,128)S(1)}, u32[]{:S(2)}, u32[]{:S(2)}) collective-permute-start(f32[512,1152]{1,0:T(8,128)} %convolution_multiply_fusion), channel_id=1, source_target_pairs={{0,8},{8,0},{1,9},{9,1},{2,10},{10,2},{3,11},{11,3},{4,12},{12,4},... | collective-permute-start | bytes 7077896 | tf_op jit(solution)/shard_map/ppermute | solution.py:19
  72.6 2.4 copy-start.10
  75.0 2.5 copy-start.16
  77.5 180.2 %collective-permute-start.6 = (f32[512,1152]{1,0:T(8,128)}, f32[512,1152]{1,0:T(8,128)}, u32[]{:S(2)}, u32[]{:S(2)}) collective-permute-start(f32[512,1152]{1,0:T(8,128)} %convolution_multiply_fusion.1), channel_id=1, source_target_pairs={{0,4},{4,0},{1,5},{5,1},{2,6},{6,2},{3,7},{7,3},{8,12},{12,8},{9,1... | collective-permute-start | bytes 7077896 | tf_op jit(solution)/shard_map/ppermute | solution.py:19
  80.7 2.4 copy-start.3
  83.1 2.4 copy-start.7
  85.6 172.1 %collective-permute-start.5 = (f32[512,1152]{1,0:T(8,128)}, f32[512,1152]{1,0:T(8,128)}, u32[]{:S(2)}, u32[]{:S(2)}) collective-permute-start(f32[512,1152]{1,0:T(8,128)} %convolution_multiply_fusion.2), channel_id=1, source_target_pairs={{0,2},{2,0},{1,3},{3,1},{4,6},{6,4},{5,7},{7,5},{8,10},{10,8},{9,1... | collective-permute-start | bytes 7077896 | tf_op jit(solution)/shard_map/ppermute | solution.py:19
  86.3 2.4 copy-start.11
  88.7 2.4 copy-start.14
  91.1 166.6 %collective-permute-start.4 = (f32[512,1152]{1,0:T(8,128)}, f32[512,1152]{1,0:T(8,128)}, u32[]{:S(2)}, u32[]{:S(2)}) collective-permute-start(f32[512,1152]{1,0:T(8,128)} %convolution_multiply_fusion.3), channel_id=1, source_target_pairs={{0,1},{1,0},{2,3},{3,2},{4,5},{5,4},{6,7},{7,6},{8,9},{9,8},{10,11... | collective-permute-start | bytes 7077896 | tf_op jit(solution)/shard_map/ppermute | solution.py:19
  249.5 2.7 %copy-start.12 = (bf16[512,1152]{1,0:T(8,128)(2,1)S(1)}, bf16[512,1152]{1,0:T(8,128)(2,1)}, u32[]{:S(2)}) copy-start(bf16[512,1152]{1,0:T(8,128)(2,1)} %copy-done.11) | copy-start | bytes 3538948
  249.5 2.7 %copy-start.13 = (f32[512,1152]{1,0:T(8,128)S(1)}, f32[512,1152]{1,0:T(8,128)}, u32[]{:S(2)}) copy-start(f32[512,1152]{1,0:T(8,128)} %fusion.37) | copy-start | bytes 7077892
  249.5 3.0 %copy-start.15 = (f32[512,512]{1,0:T(8,128)S(1)}, f32[512,512]{1,0:T(8,128)}, u32[]{:S(2)}) copy-start(f32[512,512]{1,0:T(8,128)} %copy-done.14) | copy-start | bytes 3145732
  252.4 1.7 copy-start.2
  252.4 2.0 copy-start.4
  252.4 2.3 copy-start.8
  255.8 1.9 copy-start.1
  255.8 2.0 copy-start.6
where the time goes:
time: 268 us; the launch traced here: 265 us
  blocking collectives  144 us (54%)
  waiting for transfers between devices  39.3 us (15%)
  matrix products  36.7 us (14%)
  starting transfers between devices  21.6 us (8%)
  between operations  11.5 us (4%)
  other arithmetic  9.85 us (4%)
    psum x1, blocking collectives, per_device(): lax.psum((loss_sum, scale_sum, bias_sum), ('wide', 'narrow'))  144 us
    ppermute x8, waiting for transfers between devices, from_partner(): return lax.ppermute(block, axis, route)  39.3 us
    ppermute x8, starting transfers between devices, from_partner(): return lax.ppermute(block, axis, route)  21.6 us
    dot_general x5, matrix products, text_side(): lax.dot_general(slope_cast, image_part, (((0,), (0,)), ((), ())), preferr...  14.8 us
    dot_general x5, matrix products, pair_block(): lax.dot_general(image_part, text_part, (((1,), (1,)), ((), ())), preferre...  12.2 us
    dot_general x5, matrix products, image_side(): jnp.dot(slope_cast, text_part, preferred_element_type=jnp.float32)  9.71 us
  transfers between devices with their start and end apart: 8, of which 1 were waited for; matrix products, arithmetic and copies ran while one was open for 14% of the time, Pallas kernels for 0%

commit v1 on v0

v1 whole, which is shorter than its diff:
```python
import functools

import jax
import jax.numpy as jnp
from jax import lax
from jax.experimental import pallas as pl
from jax.experimental.pallas import tpu as pltpu
from jax.sharding import PartitionSpec as P

EPS = 1e-06
MESH = pl.DeviceIdType.MESH
CHUNK = 128
CORE, NEAR, FAR, LONG = range(4)


def flip(value, *bits):
    for bit in bits:
        value = value + bit - 2 * bit * ((value // bit) % 2)
    return value


def inverse_norm(values):
    return lax.rsqrt(jnp.sum(values * values, axis=-1, keepdims=True) + EPS)


def fold(values):
    return jnp.sum(values.reshape(-1, 8, values.shape[-1]), axis=0)


def loss_and_slope(score):
    small = jnp.exp(-jnp.abs(score))
    loss = jnp.maximum(score, 0.0) + jnp.log1p(small)
    slope = jnp.where(score >= 0.0, 1.0, small) / (1.0 + small)
    return loss, slope


def kernel(
    rows,
    image_ref,
    text_ref,
    labels_ref,
    scale_ref,
    bias_ref,
    image_out,
    text_out,
    totals_out,
    arrived,
    raw,
    cast,
    inverse,
    total,
    unit,
    stats,
    sums,
    heard,
    load_sem,
    store_sem,
    send_sem,
    recv_sem,
    sum_send,
    sum_recv,
):
    parts = rows // CHUNK
    steps = 2 * parts
    wide, narrow = lax.axis_index("wide"), lax.axis_index("narrow")
    core = (wide, flip(narrow, 1))
    near = (wide, flip(narrow, 2))
    across = (wide, flip(narrow, 2, 4))
    far = (wide, flip(narrow, 8))
    others = [
        (flip(wide, 1), narrow),
        (flip(wide, 2), narrow),
        (flip(wide, 4), narrow),
        (flip(wide, 4, 8), narrow),
    ]
    friends = [core, near, across, far] + others

    barrier = pltpu.get_barrier_semaphore()
    for friend in friends:
        pl.semaphore_signal(barrier, inc=1, device_id=friend, device_id_type=MESH)
    pl.semaphore_wait(barrier, len(friends))

    scale_value = scale_ref[0]
    bias_value = bias_ref[0]
    sides = (text_ref, image_ref)

    def outgoing(route, side, part, device):
        slot = side * parts + part
        return pltpu.make_async_remote_copy(
            src_ref=sides[side].at[pl.ds(pl.multiple_of(part * CHUNK, CHUNK), CHUNK)],
            dst_ref=arrived.at[route, slot],
            send_sem=send_sem.at[route, slot],
            recv_sem=recv_sem.at[route, slot],
            device_id=device,
            device_id_type=MESH,
        )

    def relay(slot):
        return pltpu.make_async_remote_copy(
            src_ref=arrived.at[NEAR, slot],
            dst_ref=arrived.at[FAR, slot],
            send_sem=send_sem.at[FAR, slot],
            recv_sem=recv_sem.at[FAR, slot],
            device_id=across,
            device_id_type=MESH,
        )

    for route, device in ((LONG, far), (NEAR, near), (CORE, core)):
        for side in range(2):
            for part in range(parts):
                outgoing(route, side, part, device).start()

    loads = [
        pltpu.make_async_copy(ref, raw.at[side], load_sem.at[side])
        for side, ref in enumerate((image_ref, text_ref))
    ]
    for load in loads:
        load.start()
    for load in loads:
        load.wait()

    stats[...] = jnp.zeros_like(stats)

    def prepare(index, carry):
        side, part = index // parts, index % parts
        where = pl.ds(pl.multiple_of(part * CHUNK, CHUNK), CHUNK)
        values = raw[side, where, :].astype(jnp.float32)
        scaling = inverse_norm(values)
        inverse[side, where, :] = scaling
        cast[side, where, :] = (values * scaling).astype(jnp.bfloat16)
        return carry

    lax.fori_loop(0, steps, prepare, 0)

    def note(side, loss, slope, cosine):
        stats[side, 0] += fold(loss)
        stats[side, 1] += fold(slope * cosine)
        stats[side, 2] += fold(slope)

    def own(part, carry):
        where = pl.ds(pl.multiple_of(part * CHUNK, CHUNK), CHUNK)
        block = cast[0, where, :]
        cosine = lax.dot_general(
            cast[1], block, (((1,), (1,)), ((), ())), preferred_element_type=jnp.float32
        )
        logit = scale_value * cosine + bias_value
        positive = labels_ref[:, where] == lax.broadcasted_iota(jnp.int32, cosine.shape, 0)
        loss, slope = loss_and_slope(jnp.where(positive, -logit, logit))
        slope = jnp.where(positive, -slope, slope)
        note(0, loss, slope, cosine)
        slope_cast = slope.astype(jnp.bfloat16)
        term = jnp.dot(slope_cast, block, preferred_element_type=jnp.float32)

        @pl.when(part == 0)
        def _():
            total[1] = term

        @pl.when(part > 0)
        def _():
            total[1] += term

        total[0, where, :] = lax.dot_general(
            slope_cast, cast[1], (((0,), (0,)), ((), ())), preferred_element_type=jnp.float32
        )
        return carry

    lax.fori_loop(0, parts, own, 0)

    def meet(route, slot):
        side = slot // parts
        values = arrived[route, slot].astype(jnp.float32)
        unit[...] = (values * inverse_norm(values)).astype(jnp.bfloat16)
        cosine = lax.dot_general(
            cast[side], unit[...], (((1,), (1,)), ((), ())), preferred_element_type=jnp.float32
        )
        loss, slope = loss_and_slope(scale_value * cosine + bias_value)
        note(side, loss, slope, cosine)
        total[side] += jnp.dot(
            slope.astype(jnp.bfloat16), unit[...], preferred_element_type=jnp.float32
        )

    def incoming(route, slot):
        return pltpu.make_async_remote_copy(
            src_ref=arrived.at[route, slot],
            dst_ref=arrived.at[route, slot],
            send_sem=send_sem.at[route, slot],
            recv_sem=recv_sem.at[route, slot],
            device_id=core,
            device_id_type=MESH,
        )

    def from_core(slot, carry):
        incoming(CORE, slot).wait_recv()
        meet(CORE, slot)
        return carry

    lax.fori_loop(0, steps, from_core, 0)

    def first_half(step, carry):
        for half in range(2):
            slot = 2 * step + half
            incoming(NEAR, slot).wait_recv()
            relay(slot).start()
            meet(NEAR, slot)
        incoming(LONG, step).wait_recv()
        meet(LONG, step)
        for half in range(2):
            slot = 2 * step + half
            incoming(FAR, slot).wait_recv()
            meet(FAR, slot)
        return carry

    lax.fori_loop(0, parts, first_half, 0)

    def finish(side, out_ref):
        def body(part, carry):
            where = pl.ds(pl.multiple_of(part * CHUNK, CHUNK), CHUNK)
            scaling = inverse[side, where, :]
            rows_unit = raw[side, where, :].astype(jnp.float32) * scaling
            gradient = scale_value * total[side, where, :]
            along = jnp.sum(rows_unit * gradient, axis=-1, keepdims=True)
            total[side, where, :] = (gradient - rows_unit * along) * scaling
            pltpu.make_async_copy(
                total.at[side, where], out_ref.at[where], store_sem.at[side, part]
            ).start()
            return carry

        lax.fori_loop(0, parts, body, 0)

    sums[0] = stats[0]
    for stage, friend in enumerate(friends):
        exchange = pltpu.make_async_remote_copy(
            src_ref=sums.at[stage],
            dst_ref=heard.at[stage],
            send_sem=sum_send.at[stage],
            recv_sem=sum_recv.at[stage],
            device_id=friend,
            device_id_type=MESH,
        )
        exchange.start()
        if stage == 0:
            finish(0, image_out)
        exchange.wait()
        sums[stage + 1] = sums[stage] + heard[stage]

    def second_half(step, carry):
        incoming(LONG, step).wait_recv()
        meet(LONG, step)
        return carry

    lax.fori_loop(parts, steps, second_half, 0)
    finish(1, text_out)

    count = rows * lax.axis_size(("wide", "narrow"))
    for index in range(3):
        totals_out[index] = jnp.sum(sums[len(friends), index]) / count

    def drain(slot, carry):
        for route in (CORE, NEAR, FAR, LONG):
            incoming(route, slot).wait_send()
        return carry

    lax.fori_loop(0, steps, drain, 0)

    def stored(part, carry):
        where = pl.ds(pl.multiple_of(part * CHUNK, CHUNK), CHUNK)
        for side, out_ref in enumerate((image_out, text_out)):
            pltpu.make_async_copy(
                total.at[side, where], out_ref.at[where], store_sem.at[side, part]
            ).wait()
        return carry

    lax.fori_loop(0, parts, stored, 0)


def per_device(image_rows, text_rows, labels, scale, bias):
    rows, width = image_rows.shape
    parts = rows // CHUNK
    gradient = jax.ShapeDtypeStruct((rows, width), jnp.float32)
    dma = pltpu.SemaphoreType.DMA
    anywhere = pl.BlockSpec(memory_space=pl.ANY)
    scalars = pl.BlockSpec(memory_space=pltpu.SMEM)
    products = 20 * rows * rows * width
    return pl.pallas_call(
        functools.partial(kernel, rows),
        out_shape=(gradient, gradient, jax.ShapeDtypeStruct((3,), jnp.float32)),
        in_specs=[
            anywhere,
            anywhere,
            pl.BlockSpec(memory_space=pltpu.VMEM),
            scalars,
            scalars,
        ],
        out_specs=(anywhere, anywhere, scalars),
        scratch_shapes=[
            pltpu.VMEM((4, 2 * parts, CHUNK, width), jnp.bfloat16),
            pltpu.VMEM((2, rows, width), jnp.bfloat16),
            pltpu.VMEM((2, rows, width), jnp.bfloat16),
            pltpu.VMEM((2, rows, 1), jnp.float32),
            pltpu.VMEM((2, rows, width), jnp.float32),
            pltpu.VMEM((CHUNK, width), jnp.bfloat16),
            pltpu.VMEM((2, 3, 8, CHUNK), jnp.float32),
            pltpu.VMEM((9, 3, 8, CHUNK), jnp.float32),
            pltpu.VMEM((8, 3, 8, CHUNK), jnp.float32),
            dma((2,)),
            dma((2, parts)),
            dma((4, 2 * parts)),
            dma((4, 2 * parts)),
            dma((8,)),
            dma((8,)),
        ],
        compiler_params=pltpu.CompilerParams(
            collective_id=0, has_side_effects=True, vmem_limit_bytes=56 << 20
        ),
        cost_estimate=pl.CostEstimate(
            flops=2 * products, bytes_accessed=16 * rows * width, transcendentals=8 * rows * rows
        ),
        name="contrast",
    )(image_rows, text_rows, labels.reshape(1, rows), scale, bias)


def solution(mesh):
    split = P(("wide", "narrow"), None)
    return jax.shard_map(
        per_device,
        mesh=mesh,
        in_specs=(split, split, P(("wide", "narrow")), P(), P()),
        out_specs=(split, split, P()),
        check_vma=False,
    )
```

time: 268 us -> 142 us (0.53); the launches traced: 265 us -> 142 us
  blocking collectives: 144 us -> 0 us
  Pallas kernels: 0 us -> 135 us
  waiting for transfers between devices: 39.3 us -> 0 us
  matrix products: 36.7 us -> 0 us
  starting transfers between devices: 21.6 us -> 0 us
  other arithmetic: 9.85 us -> 0 us
  between operations: 11.5 us -> 1.94 us
  local copies, waits for them, and re-layouts: 1.79 us -> 5.3 us
    psum x1 -> x0, blocking collectives: 144 us -> none  [per_device(): lax.psum((loss_sum, scale_sum, bias_sum), ('wide', 'narrow'))]
    pallas_call x0 -> x1, Pallas kernels: none -> 135 us  [per_device(): pl.pallas_call(functools.partial(kernel, rows), out_shape=(gradient, grad...]
    ppermute x8 -> x0, waiting for transfers between devices: 39.3 us -> none  [from_partner(): return lax.ppermute(block, axis, route)]
    dot_general x15 -> x0, matrix products: 36.7 us -> none  [the longest x5 14.8 us: text_side(): lax.dot_general(slope_cast, image_part, (((0,), (0,)), ((), ())), preferr...]
    ppermute x8 -> x0, starting transfers between devices: 21.6 us -> none  [from_partner(): return lax.ppermute(block, axis, route)]
    mul x2 -> x0, other arithmetic: 3.74 us -> none  [the longest x1 1.88 us: per_device(): (text_acc - text_unit * jnp.sum(text_unit * text_acc, axis=-1, keepdims=T...]
    unnamed x34 -> x7, local copies, waits for them, and re-layouts: 1.79 us -> 5.3 us
  transfers between devices with their start and end apart: 8 -> 0, of which waited for: 1 -> 0; matrix products, arithmetic and copies ran while one was open for 14% -> 0% of each run, Pallas kernels for 0% -> 0%
where the time goes in v1:
time: 142 us
  Pallas kernels  135 us (95%)
  local copies, waits for them, and re-layouts  5.3 us (4%)
  between operations  1.94 us (1%)
    pallas_call x1, Pallas kernels, per_device(): pl.pallas_call(functools.partial(kernel, rows), out_shape=(gradient, grad...  135 us
    unnamed x7, local copies, waits for them, and re-layouts  5.3 us

profile of v1, /device:TPU:2, one launch (start us, length us, event | category | flops | bytes accessed | tf_op | source)
XLA Modules:
  0.0 142.3 jit_solution(13317784570101903974)
XLA Ops:
  1.9 135.1 %contrast.1 = (f32[512,1152]{1,0:T(8,128)}, f32[512,1152]{1,0:T(8,128)}, f32[3]{0:T(128)}) custom-call(bf16[512,1152]{1,0:T(8,128)(2,1)} %image_ref.1, bf16[512,1152]{1,0:T(8,128)(2,1)} %text_ref.1, s32[1,512]{1,0:T(1,128)} %bitcast.1, f32[1]{0:T(128)S(6)} %copy.11.scale_ref, f32[1]{0:T(128)S(6)} %copy.12.bias_ref), custom_call_target="tpu_custom_call" | custom-call | flops 12079595520 | bytes 9437184 | tf_op jit(solution)/shard_map/contrast/pallas_call | solution.py:284
  137.0 0.0 copy-start
  137.0 3.4 %copy.13 = f32[512,1152]{1,0:T(8,128)} copy(f32[512,1152]{1,0:T(8,128)} %get-tuple-element.6) | data formatting | bytes 4718592
  140.4 0.0 copy-done
  140.4 0.0 copy-start.1
  140.4 1.4 copy.14
  141.8 0.0 copy-done.1
  141.8 0.5 copy.15
Async XLA Ops:
  137.0 3.4 %copy-start = (f32[512,1152]{1,0:T(8,128)S(1)}, f32[512,1152]{1,0:T(8,128)}, u32[]{:S(2)}) copy-start(f32[512,1152]{1,0:T(8,128)} %get-tuple-element.7) | copy-start | bytes 7077892
  140.4 1.4 copy-start.1

commit v2 on v1

v2 whole, which is shorter than its diff:
```python
import functools

import jax
import jax.numpy as jnp
from jax import lax
from jax.experimental import pallas as pl
from jax.experimental.pallas import tpu as pltpu
from jax.sharding import PartitionSpec as P

EPS = 1e-06
MESH = pl.DeviceIdType.MESH
CHUNK = 128
CORE, NEAR, FAR, LONG = range(4)


def flip(value, *bits):
    for bit in bits:
        value = value + bit - 2 * bit * ((value // bit) % 2)
    return value


def inverse_norm(values):
    return lax.rsqrt(jnp.sum(values * values, axis=-1, keepdims=True) + EPS)


def project(unit, gradient):
    return gradient - unit * jnp.sum(unit * gradient, axis=-1, keepdims=True)


def fold(values):
    return jnp.sum(values.reshape(-1, 8, values.shape[-1]), axis=0)


def loss_and_slope(score):
    small = jnp.exp(-jnp.abs(score))
    loss = jnp.maximum(score, 0.0) + jnp.log1p(small)
    slope = jnp.where(score >= 0.0, 1.0, small) / (1.0 + small)
    return loss, slope


def exchange_kernel(
    rows,
    image_ref,
    text_ref,
    labels_ref,
    scale_ref,
    bias_ref,
    total,
    raw,
    inverse,
    sums_out,
    arrived,
    cast,
    labels,
    scale_here,
    bias_here,
    unit,
    stats,
    sums,
    heard,
    levels,
    load_sem,
    send_sem,
    recv_sem,
    sum_send,
    sum_recv,
    level_send,
    level_recv,
):
    parts = rows // CHUNK
    steps = 2 * parts
    wide, narrow = lax.axis_index("wide"), lax.axis_index("narrow")
    core = (wide, flip(narrow, 1))
    near = (wide, flip(narrow, 2))
    across = (wide, flip(narrow, 2, 4))
    far = (wide, flip(narrow, 8))
    plane = [core, near, across, (flip(wide, 4), narrow), (flip(wide, 4, 8), narrow)]
    level = narrow // 8 * 4 + wide % 4
    column = [
        ((flip(wide, *low), flip(narrow, *high)), flip(level, *low, *(4 for _ in high)))
        for high in ((8,), ())
        for low in ((), (1,), (2,), (1, 2))
        if high or low
    ]
    friends = plane + [device for device, _ in column]

    barrier = pltpu.get_barrier_semaphore()
    for friend in friends:
        pl.semaphore_signal(barrier, inc=1, device_id=friend, device_id_type=MESH)

    loads = [
        pltpu.make_async_copy(source, target, load_sem.at[index])
        for index, (source, target) in enumerate(
            (
                (image_ref, raw.at[0]),
                (text_ref, raw.at[1]),
                (labels_ref, labels),
                (scale_ref, scale_here),
                (bias_ref, bias_here),
            )
        )
    ]
    for load in loads:
        load.start()

    pl.semaphore_wait(barrier, len(friends))

    sides = (text_ref, image_ref)

    def outgoing(route, side, part, device):
        slot = side * parts + part
        return pltpu.make_async_remote_copy(
            src_ref=sides[side].at[pl.ds(pl.multiple_of(part * CHUNK, CHUNK), CHUNK)],
            dst_ref=arrived.at[route, slot],
            send_sem=send_sem.at[route, slot],
            recv_sem=recv_sem.at[route, slot],
            device_id=device,
            device_id_type=MESH,
        )

    def relay(slot):
        return pltpu.make_async_remote_copy(
            src_ref=arrived.at[NEAR, slot],
            dst_ref=arrived.at[FAR, slot],
            send_sem=send_sem.at[FAR, slot],
            recv_sem=recv_sem.at[FAR, slot],
            device_id=across,
            device_id_type=MESH,
        )

    for route, device in ((LONG, far), (NEAR, near), (CORE, core)):
        for side in range(2):
            for part in range(parts):
                outgoing(route, side, part, device).start()

    for load in loads:
        load.wait()
    scale_value = scale_here[0]
    bias_value = bias_here[0]
    stats[...] = jnp.zeros_like(stats)

    def prepare(index, carry):
        side, part = index // parts, index % parts
        where = pl.ds(pl.multiple_of(part * CHUNK, CHUNK), CHUNK)
        values = raw[side, where, :].astype(jnp.float32)
        scaling = inverse_norm(values)
        inverse[side, where, :] = scaling
        cast[side, where, :] = (values * scaling).astype(jnp.bfloat16)
        return carry

    lax.fori_loop(0, steps, prepare, 0)

    def note(side, loss, slope, cosine):
        stats[side, 0] += fold(loss)
        stats[side, 1] += fold(slope * cosine)
        stats[side, 2] += fold(slope)

    def own(part, carry):
        where = pl.ds(pl.multiple_of(part * CHUNK, CHUNK), CHUNK)
        block = cast[0, where, :]
        cosine = lax.dot_general(
            cast[1], block, (((1,), (1,)), ((), ())), preferred_element_type=jnp.float32
        )
        logit = scale_value * cosine + bias_value
        positive = labels[:, where] == lax.broadcasted_iota(jnp.int32, cosine.shape, 0)
        loss, slope = loss_and_slope(jnp.where(positive, -logit, logit))
        slope = jnp.where(positive, -slope, slope)
        note(0, loss, slope, cosine)
        slope_cast = slope.astype(jnp.bfloat16)
        term = jnp.dot(slope_cast, block, preferred_element_type=jnp.float32)

        @pl.when(part == 0)
        def _():
            total[1] = term

        @pl.when(part > 0)
        def _():
            total[1] += term

        total[0, where, :] = lax.dot_general(
            slope_cast, cast[1], (((0,), (0,)), ((), ())), preferred_element_type=jnp.float32
        )
        return carry

    lax.fori_loop(0, parts, own, 0)

    def meet(route, slot):
        side = slot // parts
        values = arrived[route, slot].astype(jnp.float32)
        unit[...] = (values * inverse_norm(values)).astype(jnp.bfloat16)
        cosine = lax.dot_general(
            cast[side], unit[...], (((1,), (1,)), ((), ())), preferred_element_type=jnp.float32
        )
        loss, slope = loss_and_slope(scale_value * cosine + bias_value)
        note(side, loss, slope, cosine)
        total[side] += jnp.dot(
            slope.astype(jnp.bfloat16), unit[...], preferred_element_type=jnp.float32
        )

    def incoming(route, slot):
        return pltpu.make_async_remote_copy(
            src_ref=arrived.at[route, slot],
            dst_ref=arrived.at[route, slot],
            send_sem=send_sem.at[route, slot],
            recv_sem=recv_sem.at[route, slot],
            device_id=core,
            device_id_type=MESH,
        )

    def from_core(slot, carry):
        incoming(CORE, slot).wait_recv()
        meet(CORE, slot)
        return carry

    lax.fori_loop(0, steps, from_core, 0)

    def along_y(slot, carry):
        incoming(NEAR, slot).wait_recv()
        relay(slot).start()
        meet(NEAR, slot)

        @pl.when(slot > 0)
        def _():
            incoming(FAR, slot - 1).wait_recv()
            meet(FAR, slot - 1)

        return carry

    lax.fori_loop(0, steps, along_y, 0)
    incoming(FAR, steps - 1).wait_recv()
    meet(FAR, steps - 1)

    def along_z(slot, carry):
        incoming(LONG, slot).wait_recv()
        meet(LONG, slot)
        return carry

    lax.fori_loop(0, parts, along_z, 0)

    def exchange(stage):
        return pltpu.make_async_remote_copy(
            src_ref=sums.at[stage],
            dst_ref=heard.at[stage],
            send_sem=sum_send.at[stage],
            recv_sem=sum_recv.at[stage],
            device_id=plane[stage],
            device_id_type=MESH,
        )

    def tell(index, slot):
        return pltpu.make_async_remote_copy(
            src_ref=sums.at[len(plane)],
            dst_ref=levels.at[slot],
            send_sem=level_send.at[index],
            recv_sem=level_recv.at[slot],
            device_id=column[index][0],
            device_id_type=MESH,
        )

    sums[0] = jnp.zeros_like(sums[0])
    sums[0, pl.ds(0, 3)] = jnp.sum(stats[0], axis=1)
    exchange(0).start()

    def finish_image(part, carry):
        where = pl.ds(pl.multiple_of(part * CHUNK, CHUNK), CHUNK)
        scaling = inverse[0, where, :]
        rows_unit = raw[0, where, :].astype(jnp.float32) * scaling
        total[0, where, :] = project(rows_unit, scale_value * total[0, where, :]) * scaling
        return carry

    for stage in range(len(plane)):
        exchange(stage).wait()
        sums[stage + 1] = sums[stage] + heard[stage]
        if stage + 1 < len(plane):
            exchange(stage + 1).start()
    for index in range(len(column)):
        tell(index, level).start()
    levels[level] = sums[len(plane)]
    lax.fori_loop(0, parts, finish_image, 0)

    lax.fori_loop(parts, steps, along_z, 0)

    for index, (_, slot) in enumerate(column):
        tell(index, slot).wait_recv()
    answer = levels[0]
    for index in range(1, len(column) + 1):
        answer += levels[index]
    sums_out[0] = answer
    sums_out[1] = jnp.full(answer.shape, scale_value, jnp.float32)
    for index in range(len(column)):
        tell(index, level).wait_send()

    def drain(slot, carry):
        for route in (CORE, NEAR, FAR, LONG):
            incoming(route, slot).wait_send()
        return carry

    lax.fori_loop(0, steps, drain, 0)


def finish_kernel(count, total, raw, inverse, sums, image_out, text_out, totals_out, done, sem):
    rows = total.shape[1]
    parts = rows // CHUNK
    image_copy = pltpu.make_async_copy(total.at[0], image_out, sem.at[parts])
    image_copy.start()
    scale_value = sums[1, 0:1, 0:1]

    def store(part):
        where = pl.ds(pl.multiple_of(part * CHUNK, CHUNK), CHUNK)
        return pltpu.make_async_copy(done.at[where], text_out.at[where], sem.at[part])

    def body(part, carry):
        where = pl.ds(pl.multiple_of(part * CHUNK, CHUNK), CHUNK)
        scaling = inverse[1, where, :]
        rows_unit = raw[1, where, :].astype(jnp.float32) * scaling
        done[where, :] = project(rows_unit, scale_value * total[1, where, :]) * scaling
        store(part).start()
        return carry

    lax.fori_loop(0, parts, body, 0)
    for index in range(3):
        totals_out[index] = jnp.sum(sums[0, index]) / count
    for part in range(parts):
        store(part).wait()
    image_copy.wait()


def per_device(image_rows, text_rows, labels, scale, bias):
    rows, width = image_rows.shape
    parts = rows // CHUNK
    dma = pltpu.SemaphoreType.DMA
    anywhere = pl.BlockSpec(memory_space=pl.ANY)
    here = pl.BlockSpec(memory_space=pltpu.VMEM)
    products = 20 * rows * rows * width
    held = pl.pallas_call(
        functools.partial(exchange_kernel, rows),
        out_shape=(
            pltpu.VMEM((2, rows, width), jnp.float32),
            pltpu.VMEM((2, rows, width), jnp.bfloat16),
            pltpu.VMEM((2, rows, 1), jnp.float32),
            pltpu.VMEM((2, 8, CHUNK), jnp.float32),
        ),
        in_specs=[pl.BlockSpec(memory_space=pltpu.HBM)] * 5,
        out_specs=(here,) * 4,
        scratch_shapes=[
            pltpu.VMEM((4, 2 * parts, CHUNK, width), jnp.bfloat16),
            pltpu.VMEM((2, rows, width), jnp.bfloat16),
            pltpu.VMEM((1, rows), jnp.int32),
            pltpu.SMEM((1,), jnp.float32),
            pltpu.SMEM((1,), jnp.float32),
            pltpu.VMEM((CHUNK, width), jnp.bfloat16),
            pltpu.VMEM((2, 3, 8, CHUNK), jnp.float32),
            pltpu.VMEM((6, 8, CHUNK), jnp.float32),
            pltpu.VMEM((5, 8, CHUNK), jnp.float32),
            pltpu.VMEM((8, 8, CHUNK), jnp.float32),
            dma((5,)),
            dma((4, 2 * parts)),
            dma((4, 2 * parts)),
            dma((5,)),
            dma((5,)),
            dma((7,)),
            dma((8,)),
        ],
        compiler_params=pltpu.CompilerParams(
            collective_id=0, has_side_effects=True, vmem_limit_bytes=46 << 20
        ),
        cost_estimate=pl.CostEstimate(
            flops=2 * products, bytes_accessed=8 * rows * width, transcendentals=8 * rows * rows
        ),
        name="exchange",
    )(image_rows, text_rows, labels.reshape(1, rows), scale, bias)
    gradient = jax.ShapeDtypeStruct((rows, width), jnp.float32)
    return pl.pallas_call(
        functools.partial(finish_kernel, rows * lax.axis_size(("wide", "narrow"))),
        out_shape=(gradient, gradient, jax.ShapeDtypeStruct((3,), jnp.float32)),
        in_specs=[here] * 4,
        out_specs=(anywhere, anywhere, pl.BlockSpec(memory_space=pltpu.SMEM)),
        scratch_shapes=[pltpu.VMEM((rows, width), jnp.float32), dma((parts + 1,))],
        compiler_params=pltpu.CompilerParams(vmem_limit_bytes=16 << 20),
        name="finish",
    )(*held)


def solution(mesh):
    split = P(("wide", "narrow"), None)
    return jax.shard_map(
        per_device,
        mesh=mesh,
        in_specs=(split, split, P(("wide", "narrow")), P(), P()),
        out_specs=(split, split, P()),
        check_vma=False,
    )
```

time: 142 us -> 121 us (0.85)
  Pallas kernels: 135 us -> 118 us
  local copies, waits for them, and re-layouts: 5.3 us -> 0.67 us
    pallas_call x1 -> x2, Pallas kernels: 135 us -> 118 us  [the longest x1 115 us: per_device(): pl.pallas_call(functools.partial(exchange_kernel, rows), out_shape=(pltpu...]
    unnamed x7 -> x2, local copies, waits for them, and re-layouts: 5.3 us -> 0.67 us
where the time goes in v2:
time: 121 us
  Pallas kernels  118 us (98%)
  between operations  1.94 us (2%)
    pallas_call x1, Pallas kernels, per_device(): pl.pallas_call(functools.partial(exchange_kernel, rows), out_shape=(pltpu...  115 us
    pallas_call x1, Pallas kernels, per_device(): pl.pallas_call(functools.partial(finish_kernel, rows * lax.axis_size(('wi...  2.74 us

profile of v2, /device:TPU:2, one launch (start us, length us, event | category | flops | bytes accessed | tf_op | source)
XLA Modules:
  0.0 120.8 jit_solution(706142058799310019)
XLA Ops:
  1.9 0.0 copy-start
  1.9 0.7 copy-done
  2.6 115.4 %exchange.1 = (f32[2,512,1152]{2,1,0:T(8,128)S(1)}, bf16[2,512,1152]{2,1,0:T(8,128)(2,1)S(1)}, f32[2,512,1]{2,1,0:T(8,128)S(1)}, f32[2,8,128]{2,1,0:T(8,128)S(1)}) custom-call(bf16[512,1152]{1,0:T(8,128)(2,1)} %image_ref.1, bf16[512,1152]{1,0:T(8,128)(2,1)} %text_ref.1, s32[1,512]{1,0:T(1,128)S(1)} %bitcast.1, f32[1]{0:T(128)S(6)} %copy.8.scale_ref, ...), custom_call_target="tpu_custom_call" | custom-call | flops 12079595520 | bytes 4718592 | tf_op jit(solution)/shard_map/exchange/pallas_call | solution.py:335
  118.0 2.7 %finish.1 = (f32[512,1152]{1,0:T(8,128)}, f32[512,1152]{1,0:T(8,128)}, f32[3]{0:T(128)}) custom-call(f32[2,512,1152]{2,1,0:T(8,128)S(1)} %get-tuple-element.7.total, bf16[2,512,1152]{2,1,0:T(8,128)(2,1)S(1)} %get-tuple-element.8.raw, f32[2,512,1]{2,1,0:T(8,128)S(1)} %get-tuple-element.9.inverse, f32[2,8,128]{2,1,0:T(8,128)S(1)} %get-tuple-element.10.sums), custom_call_target="tpu_custom_call" | custom-call | tf_op jit(solution)/shard_map/finish/pallas_call | solution.py:373
Async XLA Ops:
  1.9 0.7 copy-start

commit v3 on v2

--- a/solution.py
+++ b/solution.py
@@ -48,7 +48,10 @@
     total,
     raw,
     inverse,
-    sums_out,
+    levels,
+    last_slope,
+    last_unit,
+    factor,
     arrived,
     cast,
     labels,
@@ -58,7 +61,6 @@
     stats,
     sums,
     heard,
-    levels,
     load_sem,
     send_sem,
     recv_sem,
@@ -82,7 +84,7 @@
         for low in ((), (1,), (2,), (1, 2))
         if high or low
     ]
-    friends = plane + [device for device, _ in column]
+    friends = [device for device, _ in column] + plane
 
     barrier = pltpu.get_barrier_semaphore()
     for friend in friends:
@@ -184,17 +186,21 @@
 
     lax.fori_loop(0, parts, own, 0)
 
-    def meet(route, slot):
+    def slopes(route, slot, target):
         side = slot // parts
         values = arrived[route, slot].astype(jnp.float32)
-        unit[...] = (values * inverse_norm(values)).astype(jnp.bfloat16)
+        target[...] = (values * inverse_norm(values)).astype(jnp.bfloat16)
         cosine = lax.dot_general(
-            cast[side], unit[...], (((1,), (1,)), ((), ())), preferred_element_type=jnp.float32
+            cast[side], target[...], (((1,), (1,)), ((), ())), preferred_element_type=jnp.float32
         )
         loss, slope = loss_and_slope(scale_value * cosine + bias_value)
         note(side, loss, slope, cosine)
-        total[side] += jnp.dot(
-            slope.astype(jnp.bfloat16), unit[...], preferred_element_type=jnp.float32
+        return slope.astype(jnp.bfloat16)
+
+    def meet(route, slot):
+        slope_cast = slopes(route, slot, unit)
+        total[slot // parts] += jnp.dot(
+            slope_cast, unit[...], preferred_element_type=jnp.float32
         )
 
     def incoming(route, slot):
@@ -278,32 +284,51 @@
     levels[level] = sums[len(plane)]
     lax.fori_loop(0, parts, finish_image, 0)
 
-    lax.fori_loop(parts, steps, along_z, 0)
-
+    factor[...] = jnp.full(factor.shape, scale_value, jnp.float32)
+
+    def drain(slot, carry):
+        for route in (CORE, NEAR, FAR):
+            incoming(route, slot).wait_send()
+        return carry
+
+    lax.fori_loop(0, steps, drain, 0)
+
+    def along_z_sent(slot, carry):
+        incoming(LONG, slot - parts).wait_send()
+        return along_z(slot, carry)
+
+    lax.fori_loop(parts, steps - 1, along_z_sent, 0)
+    incoming(LONG, steps - 1).wait_recv()
+    last_slope[...] = slopes(LONG, steps - 1, last_unit)
+
+    for slot in range(parts - 1, steps):
+        incoming(LONG, slot).wait_send()
     for index, (_, slot) in enumerate(column):
         tell(index, slot).wait_recv()
-    answer = levels[0]
-    for index in range(1, len(column) + 1):
-        answer += levels[index]
-    sums_out[0] = answer
-    sums_out[1] = jnp.full(answer.shape, scale_value, jnp.float32)
-    for index in range(len(column)):
         tell(index, level).wait_send()
 
-    def drain(slot, carry):
-        for route in (CORE, NEAR, FAR, LONG):
-            incoming(route, slot).wait_send()
-        return carry
-
-    lax.fori_loop(0, steps, drain, 0)
-
-
-def finish_kernel(count, total, raw, inverse, sums, image_out, text_out, totals_out, done, sem):
+
+def finish_kernel(
+    count,
+    total,
+    raw,
+    inverse,
+    levels,
+    last_slope,
+    last_unit,
+    factor,
+    image_out,
+    text_out,
+    totals_out,
+    done,
+    totals,
+    sem,
+):
     rows = total.shape[1]
     parts = rows // CHUNK
     image_copy = pltpu.make_async_copy(total.at[0], image_out, sem.at[parts])
     image_copy.start()
-    scale_value = sums[1, 0:1, 0:1]
+    scale_value = factor[0:1, 0:1]
 
     def store(part):
         where = pl.ds(pl.multiple_of(part * CHUNK, CHUNK), CHUNK)
@@ -313,16 +338,23 @@
         where = pl.ds(pl.multiple_of(part * CHUNK, CHUNK), CHUNK)
         scaling = inverse[1, where, :]
         rows_unit = raw[1, where, :].astype(jnp.float32) * scaling
-        done[where, :] = project(rows_unit, scale_value * total[1, where, :]) * scaling
+        whole = total[1, where, :] + jnp.dot(
+            last_slope[where, :], last_unit[...], preferred_element_type=jnp.float32
+        )
+        done[where, :] = project(rows_unit, scale_value * whole) * scaling
         store(part).start()
         return carry
 
     lax.fori_loop(0, parts, body, 0)
+    answer = jnp.sum(levels[...], axis=0)
     for index in range(3):
-        totals_out[index] = jnp.sum(sums[0, index]) / count
+        totals[index] = jnp.sum(answer[index]) / count
+    totals_copy = pltpu.make_async_copy(totals, totals_out, sem.at[parts + 1])
+    totals_copy.start()
     for part in range(parts):
         store(part).wait()
     image_copy.wait()
+    totals_copy.wait()
 
 
 def per_device(image_rows, text_rows, labels, scale, bias):
@@ -338,10 +370,13 @@
             pltpu.VMEM((2, rows, width), jnp.float32),
             pltpu.VMEM((2, rows, width), jnp.bfloat16),
             pltpu.VMEM((2, rows, 1), jnp.float32),
-            pltpu.VMEM((2, 8, CHUNK), jnp.float32),
+            pltpu.VMEM((8, 8, CHUNK), jnp.float32),
+            pltpu.VMEM((rows, CHUNK), jnp.bfloat16),
+            pltpu.VMEM((CHUNK, width), jnp.bfloat16),
+            pltpu.VMEM((8, CHUNK), jnp.float32),
         ),
         in_specs=[pl.BlockSpec(memory_space=pltpu.HBM)] * 5,
-        out_specs=(here,) * 4,
+        out_specs=(here,) * 7,
         scratch_shapes=[
             pltpu.VMEM((4, 2 * parts, CHUNK, width), jnp.bfloat16),
             pltpu.VMEM((2, rows, width), jnp.bfloat16),
@@ -352,7 +387,6 @@
             pltpu.VMEM((2, 3, 8, CHUNK), jnp.float32),
             pltpu.VMEM((6, 8, CHUNK), jnp.float32),
             pltpu.VMEM((5, 8, CHUNK), jnp.float32),
-            pltpu.VMEM((8, 8, CHUNK), jnp.float32),
             dma((5,)),
             dma((4, 2 * parts)),
             dma((4, 2 * parts)),
@@ -362,7 +396,7 @@
             dma((8,)),
         ],
         compiler_params=pltpu.CompilerParams(
-            collective_id=0, has_side_effects=True, vmem_limit_bytes=46 << 20
+            collective_id=0, has_side_effects=True, vmem_limit_bytes=54 << 20
         ),
         cost_estimate=pl.CostEstimate(
             flops=2 * products, bytes_accessed=8 * rows * width, transcendentals=8 * rows * rows
@@ -373,10 +407,14 @@
     return pl.pallas_call(
         functools.partial(finish_kernel, rows * lax.axis_size(("wide", "narrow"))),
         out_shape=(gradient, gradient, jax.ShapeDtypeStruct((3,), jnp.float32)),
-        in_specs=[here] * 4,
-        out_specs=(anywhere, anywhere, pl.BlockSpec(memory_space=pltpu.SMEM)),
-        scratch_shapes=[pltpu.VMEM((rows, width), jnp.float32), dma((parts + 1,))],
-        compiler_params=pltpu.CompilerParams(vmem_limit_bytes=16 << 20),
+        in_specs=[here] * 7,
+        out_specs=(anywhere,) * 3,
+        scratch_shapes=[
+            pltpu.VMEM((rows, width), jnp.float32),
+            pltpu.SMEM((3,), jnp.float32),
+            dma((parts + 2,)),
+        ],
+        compiler_params=pltpu.CompilerParams(vmem_limit_bytes=24 << 20),
         name="finish",
     )(*held)
 

time: 121 us -> 120 us (level)
  no operation moved by 1% of the time
where the time goes in v3:
time: 120 us; the launch traced here: 119 us
  Pallas kernels  117 us (98%)
  between operations  1.93 us (2%)
    pallas_call x1, Pallas kernels, per_device(): pl.pallas_call(functools.partial(exchange_kernel, rows), out_shape=(pltpu...  115 us

profile of v3, /device:TPU:2, one launch (start us, length us, event | category | flops | bytes accessed | tf_op | source)
XLA Modules:
  0.0 119.3 jit_solution(12208544838208691508)
XLA Ops:
  1.9 115.0 %exchange.1 = (f32[2,512,1152]{2,1,0:T(8,128)S(1)}, bf16[2,512,1152]{2,1,0:T(8,128)(2,1)S(1)}, f32[2,512,1]{2,1,0:T(8,128)S(1)}, f32[8,8,128]{2,1,0:T(8,128)S(1)...) custom-call(bf16[512,1152]{1,0:T(8,128)(2,1)} %image_ref.1, ...), custom_call_target="tpu_custom_call" | custom-call | flops 12079595520 | bytes 4718592 | tf_op jit(solution)/shard_map/exchange/pallas_call | solution.py:367
  116.9 2.4 %finish.1 = (f32[512,1152]{1,0:T(8,128)}, f32[512,1152]{1,0:T(8,128)}, f32[3]{0:T(128)}) custom-call(f32[2,512,1152]{2,1,0:T(8,128)S(1)} %get-tuple-element.10.total, bf16[2,512,1152]{2,1,0:T(8,128)(2,1)S(1)} %get-tuple-element.11.raw, f32[2,512,1]{2,1,0:T(8,128)S(1)} %get-tuple-element.12.inverse, f32[8,8,128]{2,1,0:T(8,128)S(1)} %get-tuple-element.13.levels, ...), custom_call_target="tpu_custom_call" | custom-call | tf_op jit(solution)/shard_map/finish/pallas_call | solution.py:407

commit v4 on v3

--- a/solution.py
+++ b/solution.py
@@ -48,7 +48,7 @@
     total,
     raw,
     inverse,
-    levels,
+    answer,
     last_slope,
     last_unit,
     factor,
@@ -61,6 +61,7 @@
     stats,
     sums,
     heard,
+    levels,
     load_sem,
     send_sem,
     recv_sem,
@@ -68,6 +69,10 @@
     sum_recv,
     level_send,
     level_recv,
+    pair_in,
+    far_in,
+    go_far,
+    all_in,
 ):
     parts = rows // CHUNK
     steps = 2 * parts
@@ -78,17 +83,17 @@
     far = (wide, flip(narrow, 8))
     plane = [core, near, across, (flip(wide, 4), narrow), (flip(wide, 4, 8), narrow)]
     level = narrow // 8 * 4 + wide % 4
-    column = [
-        ((flip(wide, *low), flip(narrow, *high)), flip(level, *low, *(4 for _ in high)))
-        for high in ((8,), ())
-        for low in ((), (1,), (2,), (1, 2))
-        if high or low
+    upper = [
+        ((flip(wide, *low), far[1]), flip(level, 4, *low)) for low in ((), (1,), (2,), (1, 2))
     ]
-    friends = [device for device, _ in column] + plane
-
+    lower = [((flip(wide, *low), narrow), flip(level, *low)) for low in ((1,), (2,), (1, 2))]
+    columns = (lower, upper)
+    friends = [device for device, _ in upper + lower] + plane[1:]
+    levels[...] = jnp.zeros_like(levels)
     barrier = pltpu.get_barrier_semaphore()
-    for friend in friends:
-        pl.semaphore_signal(barrier, inc=1, device_id=friend, device_id_type=MESH)
+
+    def signal(semaphore, device):
+        pl.semaphore_signal(semaphore, inc=1, device_id=device, device_id_type=MESH)
 
     loads = [
         pltpu.make_async_copy(source, target, load_sem.at[index])
@@ -105,8 +110,6 @@
     for load in loads:
         load.start()
 
-    pl.semaphore_wait(barrier, len(friends))
-
     sides = (text_ref, image_ref)
 
     def outgoing(route, side, part, device):
@@ -130,10 +133,35 @@
             device_id_type=MESH,
         )
 
-    for route, device in ((LONG, far), (NEAR, near), (CORE, core)):
+    def send(route, device):
         for side in range(2):
             for part in range(parts):
                 outgoing(route, side, part, device).start()
+
+    @pl.when(narrow % 2 == 0)
+    def _():
+        signal(barrier, far)
+        pl.semaphore_wait(barrier, 2)
+        signal(pair_in, core)
+        signal(far_in, far)
+        send(LONG, far)
+        pl.semaphore_wait(far_in, 1)
+        signal(go_far, core)
+        pl.semaphore_wait(all_in, 1)
+
+    @pl.when(narrow % 2 == 1)
+    def _():
+        signal(barrier, core)
+        pl.semaphore_wait(pair_in, 1)
+        for friend in friends:
+            signal(barrier, friend)
+        pl.semaphore_wait(go_far, 1)
+        send(LONG, far)
+        pl.semaphore_wait(barrier, len(friends))
+        signal(all_in, core)
+
+    send(NEAR, near)
+    send(CORE, core)
 
     for load in loads:
         load.wait()
@@ -253,13 +281,13 @@
             device_id_type=MESH,
         )
 
-    def tell(index, slot):
+    def tell(device, index, slot):
         return pltpu.make_async_remote_copy(
             src_ref=sums.at[len(plane)],
             dst_ref=levels.at[slot],
             send_sem=level_send.at[index],
             recv_sem=level_recv.at[slot],
-            device_id=column[index][0],
+            device_id=device,
             device_id_type=MESH,
         )
 
@@ -279,9 +307,16 @@
         sums[stage + 1] = sums[stage] + heard[stage]
         if stage + 1 < len(plane):
             exchange(stage + 1).start()
-    for index in range(len(column)):
-        tell(index, level).start()
-    levels[level] = sums[len(plane)]
+
+    for parity, column in enumerate(columns):
+
+        @pl.when(narrow % 2 == parity)
+        def _(parity=parity, column=column):
+            for index, (device, _) in enumerate(column):
+                tell(device, index, level).start()
+            if parity == 0:
+                levels[level] = sums[len(plane)]
+
     lax.fori_loop(0, parts, finish_image, 0)
 
     factor[...] = jnp.full(factor.shape, scale_value, jnp.float32)
@@ -298,14 +333,32 @@
         return along_z(slot, carry)
 
     lax.fori_loop(parts, steps - 1, along_z_sent, 0)
+    for parity, column in enumerate(columns):
+
+        @pl.when(narrow % 2 == parity)
+        def _(column=column):
+            for index, (device, slot) in enumerate(column):
+                tell(device, index, slot).wait_recv()
+                tell(device, index, level).wait_send()
+
+    halves = len(plane) + 1
+    sums[halves] = jnp.sum(levels[...], axis=0)
+    other_half = pltpu.make_async_remote_copy(
+        src_ref=sums.at[halves],
+        dst_ref=heard.at[len(plane)],
+        send_sem=sum_send.at[len(plane)],
+        recv_sem=sum_recv.at[len(plane)],
+        device_id=core,
+        device_id_type=MESH,
+    )
+    other_half.start()
     incoming(LONG, steps - 1).wait_recv()
     last_slope[...] = slopes(LONG, steps - 1, last_unit)
 
     for slot in range(parts - 1, steps):
         incoming(LONG, slot).wait_send()
-    for index, (_, slot) in enumerate(column):
-        tell(index, slot).wait_recv()
-        tell(index, level).wait_send()
+    other_half.wait()
+    answer[...] = sums[halves] + heard[len(plane)]
 
 
 def finish_kernel(
@@ -313,7 +366,7 @@
     total,
     raw,
     inverse,
-    levels,
+    answer,
     last_slope,
     last_unit,
     factor,
@@ -346,7 +399,6 @@
         return carry
 
     lax.fori_loop(0, parts, body, 0)
-    answer = jnp.sum(levels[...], axis=0)
     for index in range(3):
         totals[index] = jnp.sum(answer[index]) / count
     totals_copy = pltpu.make_async_copy(totals, totals_out, sem.at[parts + 1])
@@ -370,7 +422,7 @@
             pltpu.VMEM((2, rows, width), jnp.float32),
             pltpu.VMEM((2, rows, width), jnp.bfloat16),
             pltpu.VMEM((2, rows, 1), jnp.float32),
-            pltpu.VMEM((8, 8, CHUNK), jnp.float32),
+            pltpu.VMEM((8, CHUNK), jnp.float32),
             pltpu.VMEM((rows, CHUNK), jnp.bfloat16),
             pltpu.VMEM((CHUNK, width), jnp.bfloat16),
             pltpu.VMEM((8, CHUNK), jnp.float32),
@@ -385,15 +437,20 @@
             pltpu.SMEM((1,), jnp.float32),
             pltpu.VMEM((CHUNK, width), jnp.bfloat16),
             pltpu.VMEM((2, 3, 8, CHUNK), jnp.float32),
+            pltpu.VMEM((7, 8, CHUNK), jnp.float32),
             pltpu.VMEM((6, 8, CHUNK), jnp.float32),
-            pltpu.VMEM((5, 8, CHUNK), jnp.float32),
+            pltpu.VMEM((8, 8, CHUNK), jnp.float32),
             dma((5,)),
             dma((4, 2 * parts)),
             dma((4, 2 * parts)),
-            dma((5,)),
-            dma((5,)),
-            dma((7,)),
+            dma((6,)),
+            dma((6,)),
+            dma((4,)),
             dma((8,)),
+            pltpu.SemaphoreType.REGULAR,
+            pltpu.SemaphoreType.REGULAR,
+            pltpu.SemaphoreType.REGULAR,
+            pltpu.SemaphoreType.REGULAR,
         ],
         compiler_params=pltpu.CompilerParams(
             collective_id=0, has_side_effects=True, vmem_limit_bytes=54 << 20

time: 120 us -> 119 us (level)
    pallas_call x1, Pallas kernels: 115 us -> 114 us  [per_device(): pl.pallas_call(functools.partial(exchange_kernel, rows), out_shape=(pltpu...]
where the time goes in v4:
time: 119 us; the launch traced here: 118 us
  Pallas kernels  116 us (97%)
  between operations  1.93 us (2%)
    pallas_call x1, Pallas kernels, per_device(): pl.pallas_call(functools.partial(exchange_kernel, rows), out_shape=(pltpu...  114 us
    pallas_call x1, Pallas kernels, per_device(): pl.pallas_call(functools.partial(finish_kernel, rows * lax.axis_size(('wi...  2.39 us

profile of v4, /device:TPU:2, one launch (start us, length us, event | category | flops | bytes accessed | tf_op | source)
XLA Modules:
  0.0 117.9 jit_solution(13518352203165765974)
XLA Ops:
  1.9 113.6 %exchange.1 = (f32[2,512,1152]{2,1,0:T(8,128)S(1)}, bf16[2,512,1152]{2,1,0:T(8,128)(2,1)S(1)}, f32[2,512,1]{2,1,0:T(8,128)S(1)}, f32[8,128]{1,0:T(8,128)S(1)}, b...) custom-call(bf16[512,1152]{1,0:T(8,128)(2,1)} %image_ref.1, ...), custom_call_target="tpu_custom_call" | custom-call | flops 12079595520 | bytes 4718592 | tf_op jit(solution)/shard_map/exchange/pallas_call | solution.py:419
  115.5 2.4 %finish.1 = (f32[512,1152]{1,0:T(8,128)}, f32[512,1152]{1,0:T(8,128)}, f32[3]{0:T(128)}) custom-call(f32[2,512,1152]{2,1,0:T(8,128)S(1)} %get-tuple-element.10.total, bf16[2,512,1152]{2,1,0:T(8,128)(2,1)S(1)} %get-tuple-element.11.raw, f32[2,512,1]{2,1,0:T(8,128)S(1)} %get-tuple-element.12.inverse, f32[8,128]{1,0:T(8,128)S(1)} %get-tuple-element.13.answer, ...), custom_call_target="tpu_custom_call" | custom-call | tf_op jit(solution)/shard_map/finish/pallas_call | solution.py:464

commit v5 on v4

--- a/solution.py
+++ b/solution.py
@@ -133,10 +133,18 @@
             device_id_type=MESH,
         )
 
-    def send(route, device):
-        for side in range(2):
-            for part in range(parts):
-                outgoing(route, side, part, device).start()
+    def send(route, device, side, count):
+        for part in range(count):
+            outgoing(route, side, part, device).start()
+
+    patient = wide % 4 >= 2
+
+    def send_far():
+        send(LONG, far, 0, parts)
+
+        @pl.when(jnp.logical_not(patient))
+        def _():
+            send(LONG, far, 1, parts)
 
     @pl.when(narrow % 2 == 0)
     def _():
@@ -144,7 +152,7 @@
         pl.semaphore_wait(barrier, 2)
         signal(pair_in, core)
         signal(far_in, far)
-        send(LONG, far)
+        send_far()
         pl.semaphore_wait(far_in, 1)
         signal(go_far, core)
         pl.semaphore_wait(all_in, 1)
@@ -156,18 +164,21 @@
         for friend in friends:
             signal(barrier, friend)
         pl.semaphore_wait(go_far, 1)
-        send(LONG, far)
+        send_far()
         pl.semaphore_wait(barrier, len(friends))
         signal(all_in, core)
 
-    send(NEAR, near)
-    send(CORE, core)
+    for side in range(2):
+        send(NEAR, near, side, parts)
+    for side in range(2):
+        send(CORE, core, side, parts)
 
     for load in loads:
         load.wait()
     scale_value = scale_here[0]
     bias_value = bias_here[0]
     stats[...] = jnp.zeros_like(stats)
+    total[...] = jnp.zeros_like(total)
 
     def prepare(index, carry):
         side, part = index // parts, index % parts
@@ -185,7 +196,7 @@
         stats[side, 1] += fold(slope * cosine)
         stats[side, 2] += fold(slope)
 
-    def own(part, carry):
+    def own(part):
         where = pl.ds(pl.multiple_of(part * CHUNK, CHUNK), CHUNK)
         block = cast[0, where, :]
         cosine = lax.dot_general(
@@ -197,22 +208,10 @@
         slope = jnp.where(positive, -slope, slope)
         note(0, loss, slope, cosine)
         slope_cast = slope.astype(jnp.bfloat16)
-        term = jnp.dot(slope_cast, block, preferred_element_type=jnp.float32)
-
-        @pl.when(part == 0)
-        def _():
-            total[1] = term
-
-        @pl.when(part > 0)
-        def _():
-            total[1] += term
-
-        total[0, where, :] = lax.dot_general(
+        total[1] += jnp.dot(slope_cast, block, preferred_element_type=jnp.float32)
+        total[0, where, :] += lax.dot_general(
             slope_cast, cast[1], (((0,), (0,)), ((), ())), preferred_element_type=jnp.float32
         )
-        return carry
-
-    lax.fori_loop(0, parts, own, 0)
 
     def slopes(route, slot, target):
         side = slot // parts
@@ -241,17 +240,14 @@
             device_id_type=MESH,
         )
 
-    def from_core(slot, carry):
-        incoming(CORE, slot).wait_recv()
-        meet(CORE, slot)
-        return carry
-
-    lax.fori_loop(0, steps, from_core, 0)
-
-    def along_y(slot, carry):
+    def along_y(with_own, slot, carry):
         incoming(NEAR, slot).wait_recv()
         relay(slot).start()
         meet(NEAR, slot)
+        if with_own:
+            own(slot)
+        incoming(CORE, slot).wait_recv()
+        meet(CORE, slot)
 
         @pl.when(slot > 0)
         def _():
@@ -260,7 +256,14 @@
 
         return carry
 
-    lax.fori_loop(0, steps, along_y, 0)
+    lax.fori_loop(0, parts, functools.partial(along_y, True), 0)
+    lax.fori_loop(parts, parts + 2, functools.partial(along_y, False), 0)
+
+    @pl.when(patient)
+    def _():
+        send(LONG, far, 1, parts)
+
+    lax.fori_loop(parts + 2, steps, functools.partial(along_y, False), 0)
     incoming(FAR, steps - 1).wait_recv()
     meet(FAR, steps - 1)
 
@@ -333,6 +336,11 @@
         return along_z(slot, carry)
 
     lax.fori_loop(parts, steps - 1, along_z_sent, 0)
+    incoming(LONG, steps - 1).wait_recv()
+    last_slope[...] = slopes(LONG, steps - 1, last_unit)
+
+    for slot in range(parts - 1, steps):
+        incoming(LONG, slot).wait_send()
     for parity, column in enumerate(columns):
 
         @pl.when(narrow % 2 == parity)
@@ -352,11 +360,6 @@
         device_id_type=MESH,
     )
     other_half.start()
-    incoming(LONG, steps - 1).wait_recv()
-    last_slope[...] = slopes(LONG, steps - 1, last_unit)
-
-    for slot in range(parts - 1, steps):
-        incoming(LONG, slot).wait_send()
     other_half.wait()
     answer[...] = sums[halves] + heard[len(plane)]
 

time: 119 us -> 120 us (level)
  no operation moved by 1% of the time
where the time goes in v5:
time: 120 us; the launch traced here: 118 us
  Pallas kernels  116 us (97%)
  between operations  2.09 us (2%)
    pallas_call x1, Pallas kernels, per_device(): pl.pallas_call(functools.partial(exchange_kernel, rows), out_shape=(pltpu...  114 us

profile of v5, /device:TPU:2, one launch (start us, length us, event | category | flops | bytes accessed | tf_op | source)
XLA Modules:
  0.0 118.1 jit_solution(7573140897838670704)
XLA Ops:
  1.9 113.6 %exchange.1 = (f32[2,512,1152]{2,1,0:T(8,128)S(1)}, bf16[2,512,1152]{2,1,0:T(8,128)(2,1)S(1)}, f32[2,512,1]{2,1,0:T(8,128)S(1)}, f32[8,128]{1,0:T(8,128)S(1)}, b...) custom-call(bf16[512,1152]{1,0:T(8,128)(2,1)} %image_ref.1, ...), custom_call_target="tpu_custom_call" | custom-call | flops 12079595520 | bytes 4718592 | tf_op jit(solution)/shard_map/exchange/pallas_call | solution.py:422
  115.5 2.4 %finish.1 = (f32[512,1152]{1,0:T(8,128)}, f32[512,1152]{1,0:T(8,128)}, f32[3]{0:T(128)}) custom-call(f32[2,512,1152]{2,1,0:T(8,128)S(1)} %get-tuple-element.10.total, bf16[2,512,1152]{2,1,0:T(8,128)(2,1)S(1)} %get-tuple-element.11.raw, f32[2,512,1]{2,1,0:T(8,128)S(1)} %get-tuple-element.12.inverse, f32[8,128]{1,0:T(8,128)S(1)} %get-tuple-element.13.answer, ...), custom_call_target="tpu_custom_call" | custom-call | tf_op jit(solution)/shard_map/finish/pallas_call | solution.py:467
